TPU v7x, 128 devices: a whole 4x4x4 slice. The times are simulated.
128 devices in a mesh: col: 4 (over x_hi, core), af: 32 (over z, x_lo, y).
Axes of the slice: x: 4 (x_hi: 2, x_lo: 2; x = x_hi * 2 + x_lo), y: 4, z: 4, core: 2. Of those that a mesh axis runs over, the one named last changes fastest.
Arguments:
- coarse_state: float32 [3, 8, 512, 1024], P(None, None, 'af', 'col'), may hold values from 0.1 to 2
- coarse_kappa: float32 [8, 512, 1024], P(None, 'af', 'col'), may hold values from 0.25 to 1
- coarse_rate: float32 [8, 512, 1024], P(None, 'af', 'col'), may hold values from 0.5 to 6
- fine_state: float32 [512, 3, 32, 1024], P(('col', 'af')), may hold values from 0.1 to 2
- fine_kappa: float32 [512, 32, 1024], P(('col', 'af')), may hold values from 0.25 to 1
- fine_rate: float32 [512, 32, 1024], P(('col', 'af')), may hold values from 0.5 to 6
- boxes: int32 [512, 2], replicated, may hold values from 0 to 127, as said below
- cover: int32 [64, 128], replicated, may hold values from -1 to 511, as said below
Outputs:
- coarse_out: float32 [3, 8, 512, 1024], P(None, None, 'af', 'col')
- fine_out: float32 [512, 3, 32, 1024], P(('col', 'af'))
Inputs may be any that keep to these rules, and one draw needn't show every extreme that they name: `boxes`: A patch's block spans all 8 planes; it lies in the 32 block rows of one col index, never in the first or last of them nor in the slab's first or last block column, and no two patches share a face. The patches whose blocks lie in one col index's rows are the rows of the fine arrays held by that col index, in no particular order. The 2 block columns of one af index hold at most 10 patches, and in every col index some af index holds exactly that many. cover[bx, by] is the patch whose block is (bx, by), or -1 where none is; it agrees with boxes, and every patch appears once.
All inputs are finite; a program needn't handle non-finite values.
Results may differ from a plain program's by a relative error of at most 0.0003.
Values sent between devices are 32-bit elements; how exact they have to be, the bound alone decides.
A program may use at most 192 MiB of HBM per device.

v0:
```python
import jax
import jax.numpy as jnp
from jax import lax
from jax.sharding import PartitionSpec as P

NZC = 8
RATIO = 4
BLK = 8
DT_COARSE = 1.0 / 28.0
DIFFUSE = (1.0, 0.7, 0.45)
NEIGHBOURS = ((1, 0, 0), (-1, 0, 0), (0, 1, 0), (0, -1, 0), (0, 0, 1), (0, 0, -1))


def with_halo(cells, sides, width):
    for axis, dim in sides:
        count = lax.axis_size(axis)
        ends = count - 1
        head = lax.slice_in_dim(cells, 0, width, axis=dim)
        tail = lax.slice_in_dim(cells, cells.shape[dim] - width, cells.shape[dim], axis=dim)
        cells = jnp.concatenate(
            [
                lax.ppermute(tail, axis, [(i, (i + 1) % count) for i in range(ends)]),
                cells,
                lax.ppermute(head, axis, [((i + 1) % count, i) for i in range(ends)]),
            ],
            axis=dim,
        )
    return cells


def harmonic(first, second):
    summed = first + second
    positive = summed > 0.0
    return jnp.where(positive, 2.0 * first * second / jnp.where(positive, summed, 1.0), 0.0)


def combine(center, conduct, neighbour_list, reaction, inv_square, step_size):
    summed = jnp.zeros_like(center)
    for values, coeffs in neighbour_list:
        summed = summed + harmonic(conduct, coeffs) * (values - center)
    spread = (
        jnp.stack([DIFFUSE[0] * summed[0], DIFFUSE[1] * summed[1], DIFFUSE[2] * summed[2]])
        * inv_square
    )
    forward = reaction * (center[0] * center[1] - center[2])
    change = spread + jnp.stack([-forward, -forward, forward])
    return center + step_size * change


def window(values, step_z, step_x, step_y):
    depth_len = values.shape[-3] - 2
    across = values.shape[-2] - 2
    along_len = values.shape[-1] - 2
    return values[
        ...,
        1 + step_z : 1 + step_z + depth_len,
        1 + step_x : 1 + step_x + across,
        1 + step_y : 1 + step_y + along_len,
    ]


def coarse_advance(padded_xy, conduct_xy, reaction):
    padded = jnp.pad(padded_xy, ((0, 0), (1, 1), (0, 0), (0, 0)))
    conduct = jnp.pad(conduct_xy, ((1, 1), (0, 0), (0, 0)))
    neighbour_list = [
        (
            window(padded, offsets[0], offsets[1], offsets[2]),
            window(conduct, offsets[0], offsets[1], offsets[2]),
        )
        for offsets in NEIGHBOURS
    ]
    return combine(
        window(padded, 0, 0, 0), window(conduct, 0, 0, 0), neighbour_list, reaction, 1.0, DT_COARSE
    )


def upsample(strips):
    return jnp.repeat(jnp.repeat(strips, RATIO, axis=-2), RATIO, axis=-1)


def patch_step(fields, conduct, reaction, strips):
    ghosts = upsample(strips)
    edge_len = ghosts.shape[-1]
    position = lax.broadcasted_iota(jnp.int32, (1, edge_len * edge_len), 1)
    column = position % edge_len
    row_pos = position // edge_len
    zero_fields = jnp.zeros_like(fields[:, :1])
    zero_conduct = jnp.zeros_like(conduct[:1])
    upward = (
        jnp.concatenate([fields[:, 1:], zero_fields], axis=1),
        jnp.concatenate([conduct[1:], zero_conduct], axis=0),
    )
    downward = (
        jnp.concatenate([zero_fields, fields[:, :-1]], axis=1),
        jnp.concatenate([zero_conduct, conduct[:-1]], axis=0),
    )
    last_row = row_pos == edge_len - 1
    first_row = row_pos == 0
    last_col = column == edge_len - 1
    first_col = column == 0
    next_x = (
        jnp.where(
            last_row, jnp.tile(ghosts[1], (1, 1, edge_len)), jnp.roll(fields, -edge_len, axis=-1)
        ),
        jnp.where(last_row, conduct, jnp.roll(conduct, -edge_len, axis=-1)),
    )
    prev_x = (
        jnp.where(
            first_row, jnp.tile(ghosts[0], (1, 1, edge_len)), jnp.roll(fields, edge_len, axis=-1)
        ),
        jnp.where(first_row, conduct, jnp.roll(conduct, edge_len, axis=-1)),
    )
    next_y = (
        jnp.where(
            last_col, jnp.repeat(ghosts[3], edge_len, axis=-1), jnp.roll(fields, -1, axis=-1)
        ),
        jnp.where(last_col, conduct, jnp.roll(conduct, -1, axis=-1)),
    )
    prev_y = (
        jnp.where(
            first_col, jnp.repeat(ghosts[2], edge_len, axis=-1), jnp.roll(fields, 1, axis=-1)
        ),
        jnp.where(first_col, conduct, jnp.roll(conduct, 1, axis=-1)),
    )
    return combine(
        fields,
        conduct,
        [upward, downward, next_x, prev_x, next_y, prev_y],
        reaction,
        float(RATIO * RATIO),
        DT_COARSE / RATIO,
    )


def restrict(fields):
    shaped = fields.reshape(3, NZC, RATIO, BLK, RATIO, BLK, RATIO)
    return jnp.mean(shaped, axis=(2, 4, 6)).reshape(-1)


def rim_rows(outer, block_cols, block_rows):
    species, planes, reach_x, cells_y = outer.shape
    padded_y = jnp.pad(outer, ((0, 0), (0, 0), (0, 0), (1, 1)))
    collected = []
    for column in range(block_cols):
        base_x = BLK * column
        lower_x = (
            outer[:, :, base_x, :].reshape(species, planes, block_rows, BLK).transpose(2, 0, 1, 3)
        )
        upper_x = (
            outer[:, :, base_x + BLK + 1, :]
            .reshape(species, planes, block_rows, BLK)
            .transpose(2, 0, 1, 3)
        )
        lower_y = padded_y[:, :, base_x + 1 : base_x + 1 + BLK, 0:cells_y:BLK].transpose(3, 0, 1, 2)
        upper_y = padded_y[
            :, :, base_x + 1 : base_x + 1 + BLK, BLK + 1 : cells_y + 2 : BLK
        ].transpose(3, 0, 1, 2)
        face_rows = jnp.stack([lower_x, upper_x, lower_y, upper_y], axis=1)
        collected.append(face_rows.reshape(block_rows, -1))
    return jnp.concatenate(collected, axis=0)


def sum_sources(received):
    return jnp.sum(received, axis=0)


def per_device(
    coarse_state, coarse_kappa, coarse_rate, fine_state, fine_kappa, fine_rate, boxes, cover
):
    af_count = lax.axis_size("af")
    af_index = lax.axis_index("af")
    col_index = lax.axis_index("col")
    slot_count = fine_state.shape[0]
    cells_x = coarse_state.shape[2]
    cells_y = coarse_state.shape[3]
    block_cols = cells_x // BLK
    block_rows = cells_y // BLK
    group_size = af_count * slot_count
    group_base = col_index * group_size
    stacked = jnp.concatenate([coarse_state, coarse_kappa[None]], axis=0)
    widened = with_halo(stacked, (("col", 3), ("af", 2)), 1)
    coarse_new = coarse_advance(widened[:3], widened[3], coarse_rate)
    outer_new = with_halo(coarse_new, (("af", 2),), 1)
    outer_old = widened[:3, :, :, 1:-1]
    group_boxes = lax.dynamic_slice_in_dim(boxes, group_base, group_size, 0)
    local_x = group_boxes[:, 0] - af_index * block_cols
    local_y = group_boxes[:, 1] - col_index * block_rows
    inside = (local_x >= 0) & (local_x < block_cols) & (local_y >= 0) & (local_y < block_rows)
    block_ids = jnp.where(inside, local_x * block_rows + local_y, -1)
    targets = (
        block_ids[:, None] == jnp.arange(block_cols * block_rows, dtype=jnp.int32)[None, :]
    ).astype(jnp.float32)
    earlier = rim_rows(outer_old, block_cols, block_rows)
    updated = rim_rows(outer_new, block_cols, block_rows)
    fields = fine_state
    for substep in range(RATIO):
        fraction = substep / RATIO
        current = earlier + fraction * (updated - earlier)
        send_rows = jnp.dot(targets, current, precision=lax.Precision.HIGHEST)
        strips = sum_sources(
            lax.all_to_all(
                send_rows.reshape(af_count, slot_count, current.shape[1]),
                "af",
                split_axis=0,
                concat_axis=0,
                tiled=True,
            )
        )
        strips = strips.reshape(slot_count, 4, 3, NZC, BLK)
        fields = jax.vmap(patch_step)(fields, fine_kappa, fine_rate, strips)
    averages = jax.vmap(restrict)(fields)
    cover_mine = lax.dynamic_slice(
        cover, (af_index * block_cols, col_index * block_rows), (block_cols, block_rows)
    ).reshape(-1)
    wanted = cover_mine - group_base
    portion = lax.all_gather(averages, "af", axis=0, tiled=True)
    selector = (wanted[:, None] == jnp.arange(portion.shape[0], dtype=jnp.int32)[None, :]).astype(
        jnp.float32
    )
    placed = jnp.dot(selector, portion, precision=lax.Precision.HIGHEST)
    placed = (
        placed.reshape(block_cols, block_rows, 3, NZC, BLK, BLK)
        .transpose(2, 3, 0, 4, 1, 5)
        .reshape(3, NZC, cells_x, cells_y)
    )
    covered = (cover_mine >= 0).reshape(block_cols, block_rows)
    covered = jnp.repeat(jnp.repeat(covered, BLK, axis=0), BLK, axis=1)
    coarse_out = jnp.where(covered[None, None], placed, coarse_new)
    return (coarse_out, fields)


def solution(mesh):
    return jax.shard_map(
        per_device,
        mesh=mesh,
        in_specs=(
            P(None, None, "af", "col"),
            P(None, "af", "col"),
            P(None, "af", "col"),
            P(("col", "af"), None, None, None),
            P(("col", "af"), None, None),
            P(("col", "af"), None, None),
            P(),
            P(),
        ),
        out_specs=(P(None, None, "af", "col"), P(("col", "af"), None, None, None)),
        check_vma=False,
    )
```

profile of v0, /device:TPU:4, one launch (start us, length us, event | category | flops | bytes accessed | tf_op | source)
XLA Modules:
  0.0 597.3 jit_solution(5692772814283135084)
XLA Ops:
  4.6 5.1 collective-permute-start.1
  31.8 4.5 compare_select_fusion.10
  46.5 3.5 collective-permute-start.2
  61.2 3.1 slice.500
  64.3 3.1 slice.503
  67.4 3.1 slice.504
  77.2 4.1 collective-permute-start.4
  104.3 3.1 slice.532
  107.4 3.1 slice.533
  124.3 12.2 %all-to-all-start = ((f32[32,4,768]{2,1,0:T(4,128)}), f32[32,4,768]{2,1,0:T(4,128)}, u32[]{:S(2)}, u32[]{:S(2)}) async-start(f32[32,4,768]{2,1,0:T(4,128)} %reshape.321), calls=%async_computation | async-start | bytes 786432 | tf_op jit(solution)/shard_map/all_to_all | solution.py:201
  146.5 8.9 %all-to-all-start.1 = ((f32[32,4,768]{2,1,0:T(4,128)}), f32[32,4,768]{2,1,0:T(4,128)}, u32[]{:S(2)}, u32[]{:S(2)}) async-start(f32[32,4,768]{2,1,0:T(4,128)} %reshape.327), calls=%async_computation.1 | async-start | bytes 786432 | tf_op jit(solution)/shard_map/all_to_all | solution.py:201
  162.3 3.7 broadcast_in_dim.329
  166.0 5.9 reshape.325
  172.0 3.7 broadcast_in_dim.332
  175.8 5.9 reshape.326
  184.8 5.9 tile.82
  193.8 6.0 %tile.85 = f32[4,3,32,1024]{3,2,0,1:T(8,128)} reshape(f32[4,3,32,32,32]{4,3,2,0,1:T(8,128)} %tile.84) | data formatting | bytes 3145728 | tf_op jit(solution)/shard_map/vmap()/tile | solution.py:109
  199.8 7.7 %fusion.5 = f32[4,3,32,1024]{3,2,0,1:T(8,128)S(1)} fusion(f32[4,3,32,1024]{3,2,0,1:T(8,128)} %tile.82, f32[4,3,32,32]{3,2,0,1:T(8,128)} %get-tuple-element.69, f32[4,3,32,992]{3,2,0,1:T(8,128)} %get-tuple-element.71, f32[4,3,32,1024]{3,2,0,1:T(8,128)} %tile.85, f32[4,3,32,992]{3,2,0,1:T(8,128)} %get-tuple-element.70, f32[4,3,32,32]{3,2,0,1:T(8,128)} %get-tuple-element.68, ...), kind=kLoop, calls=%fused_computation.8 | loop fusion | flops 9830400 | bytes 21925888 | tf_op jit(solution)/shard_map/vmap()/add | solution.py:40
  218.0 8.4 %all-to-all-start.2 = ((f32[32,4,768]{2,1,0:T(4,128)}), f32[32,4,768]{2,1,0:T(4,128)S(1)}, u32[]{:S(2)}, u32[]{:S(2)}) async-start(f32[32,4,768]{2,1,0:T(4,128)} %reshape.333), calls=%async_computation.2 | async-start | bytes 786432 | tf_op jit(solution)/shard_map/all_to_all | solution.py:201
  236.2 4.8 broadcast_in_dim.335
  241.0 5.9 reshape.331
  248.6 4.8 broadcast_in_dim.336
  253.4 5.9 reshape.332
  261.1 3.9 tile.87
  265.0 5.9 tile.88
  272.6 3.9 tile.90
  276.5 5.9 tile.91
  282.5 8.4 %fusion.21 = f32[4,3,32,1024]{3,2,0,1:T(8,128)S(1)} fusion(f32[4,3,32,1024]{3,2,0,1:T(8,128)} %tile.88, f32[4,3,32,32]{3,2,0,1:T(8,128)} %get-tuple-element.56, f32[4,3,32,992]{3,2,0,1:T(8,128)} %get-tuple-element.58, f32[4,3,32,1024]{3,2,0,1:T(8,128)} %tile.91, f32[4,3,32,992]{3,2,0,1:T(8,128)} %get-tuple-element.57, ...), kind=kLoop, calls=%fused_computation.29 | loop fusion | flops 12976128 | bytes 24547328 | tf_op jit(solution)/shard_map/vmap()/add | solution.py:40
  303.2 8.6 %all-to-all-start.3 = ((f32[32,4,768]{2,1,0:T(4,128)}), f32[32,4,768]{2,1,0:T(4,128)}, u32[]{:S(2)}, u32[]{:S(2)}) async-start(f32[32,4,768]{2,1,0:T(4,128)} %reshape.339), calls=%async_computation.3 | async-start | bytes 786432 | tf_op jit(solution)/shard_map/all_to_all | solution.py:201
  316.6 3.7 broadcast_in_dim.339
  320.4 5.9 reshape.337
  327.3 3.7 broadcast_in_dim.340
  331.0 5.9 reshape.338
  341.0 5.9 tile.94
  350.0 6.0 %tile.97 = f32[4,3,32,1024]{3,2,0,1:T(8,128)} reshape(f32[4,3,32,32,32]{4,3,2,0,1:T(8,128)} %tile.96) | data formatting | bytes 3145728 | tf_op jit(solution)/shard_map/vmap()/tile | solution.py:109
  356.1 10.2 %fusion.37 = f32[4,3,32,1024]{3,2,0,1:T(8,128)S(1)} fusion(f32[4,3,32,1024]{3,2,0,1:T(8,128)} %tile.94, f32[4,3,32,32]{3,2,0,1:T(8,128)} %get-tuple-element.43, f32[4,3,32,992]{3,2,0,1:T(8,128)} %get-tuple-element.45, f32[4,3,32,1024]{3,2,0,1:T(8,128)} %tile.97, f32[4,3,32,992]{3,2,0,1:T(8,128)} %get-tuple-element.44, ...), kind=kLoop, calls=%fused_computation.50 | loop fusion | flops 16121856 | bytes 27168768 | tf_op jit(solution)/shard_map/vmap()/add | solution.py:40
  380.6 3.7 broadcast_in_dim.343
  384.3 5.9 reshape.343
  390.3 3.7 broadcast_in_dim.344
  394.1 5.9 reshape.344
  403.1 5.9 tile.100
  412.1 6.1 %tile.103 = f32[4,3,32,1024]{3,2,0,1:T(8,128)} reshape(f32[4,3,32,32,32]{4,3,2,0,1:T(8,128)} %tile.102) | data formatting | bytes 3145728 | tf_op jit(solution)/shard_map/vmap()/tile | solution.py:109
  418.2 7.3 %fusion.50 = f32[4,3,32,1024]{3,2,0,1:T(8,128)S(1)} fusion(f32[4,3,32,1024]{3,2,0,1:T(8,128)} %tile.100, f32[4,3,32,1024]{3,2,0,1:T(8,128)} %tile.103, f32[4,3,32,1024]{3,2,0,1:T(8,128)} %reshape.343, f32[4,3,32,1024]{3,2,0,1:T(8,128)} %reshape.344, f32[4,32,1024]{2,1,0:T(8,128)} %get-tuple-element.95, f32[4,32,1024]{2,1,0:T(8,128)S(1)} %copy-done.21, ...), kind=kLoop, calls=%fused_computation.68 | loop fusion | flops 9830400 | bytes 21925888 | tf_op jit(solution)/shard_map/vmap()/add | solution.py:40
  427.1 53.4 %reshape.345 = f32[4,3,8,4,8,4,8,4]{7,6,5,4,3,2,1,0:T(8,128)} reshape(f32[4,3,32,1024]{3,2,1,0:T(8,128)S(1)} %bitcast_add_fusion) | data formatting | bytes 3145728 | tf_op jit(solution)/shard_map/vmap()/reshape | solution.py:136
  480.5 17.8 %reduce_sum.49 = f32[4,3,8,8,8]{4,3,2,1,0:T(8,128)S(1)} reduce(f32[4,3,8,4,8,4,8,4]{7,6,5,4,3,2,1,0:T(8,128)} %reshape.345, f32[]{:T(128)} %constant.94.clone.1), dimensions={3,5,7}, to_apply=%region_4.5 | reduce | flops 387072 | bytes 1597444 | tf_op jit(solution)/shard_map/vmap()/reduce_sum | solution.py:137
  498.6 85.9 %all-gather = f32[32,4,1536]{2,1,0:T(4,128)S(1)} all-gather(f32[1,4,1536]{2,1,0:T(4,128)S(1)} %reshape.348), channel_id=1, replica_groups=mesh['col'=4,'af'=32] {'af'}, dimensions={0}, use_global_device_ids=true | all-gather | bytes 811008 | tf_op jit(solution)/shard_map/all_gather | solution.py:216
  586.5 3.9 copy.314
  590.5 5.7 reshape.347
  (355 shorter events, 189.6 us)
Async XLA Ops:
  0.6 25.3 %copy-start = (s32[512,2]{0,1:T(2,128)S(1)}, s32[512,2]{0,1:T(2,128)}, u32[]{:S(2)}) copy-start(s32[512,2]{0,1:T(2,128)} %param.14) | copy-start | bytes 12292
  0.6 11.4 %copy-start.3 = (f32[4,32,1024]{2,1,0:T(8,128)S(1)}, f32[4,32,1024]{2,1,0:T(8,128)}, u32[]{:S(2)}) copy-start(f32[4,32,1024]{2,1,0:T(8,128)} %param.12) | copy-start | bytes 1572868
  2.6 41.3 %collective-permute-start = (f32[4,8,16,1]{3,2,1,0:T(8,128)}, f32[4,8,16,1]{3,2,1,0:T(8,128)}, u32[]{:S(2)}, u32[]{:S(2)}) collective-permute-start(f32[4,8,16,1]{3,2,1,0:T(8,128)} %get-tuple-element.108), channel_id=1, source_target_pairs={{0,32},{32,64},{64,96},{1,33},{33,65},{65,97},{2,34},{34,66},{66,9... | collective-permute-start | bytes 6152 | tf_op jit(solution)/shard_map/ppermute | solution.py:22
  4.6 39.4 %collective-permute-start.1 = (f32[4,8,16,1]{3,2,1,0:T(8,128)}, f32[4,8,16,1]{3,2,1,0:T(8,128)}, u32[]{:S(2)}, u32[]{:S(2)}) collective-permute-start(f32[4,8,16,1]{3,2,1,0:T(8,128)} %get-tuple-element.109), channel_id=1, source_target_pairs={{32,0},{64,32},{96,64},{33,1},{65,33},{97,65},{34,2},{66,34},{98,6... | collective-permute-start | bytes 6152 | tf_op jit(solution)/shard_map/ppermute | solution.py:24
  11.5 188.3 %copy-start.72 = (pred[1024]{0:T(1024)(128)(4,1)}, pred[1024]{0:T(1024)(128)(4,1)S(1)}, u32[]{:S(2)}) copy-start(pred[1024]{0:T(1024)(128)(4,1)S(1)} %get-tuple-element.121) | copy-start | bytes 3076
  11.5 188.3 %copy-start.75 = (pred[1024]{0:T(1024)(128)(4,1)}, pred[1024]{0:T(1024)(128)(4,1)S(1)}, u32[]{:S(2)}) copy-start(pred[1024]{0:T(1024)(128)(4,1)S(1)} %get-tuple-element.122) | copy-start | bytes 3076
  12.1 187.7 %copy-start.78 = (pred[1024]{0:T(1024)(128)(4,1)}, pred[1024]{0:T(1024)(128)(4,1)S(1)}, u32[]{:S(2)}) copy-start(pred[1024]{0:T(1024)(128)(4,1)S(1)} %get-tuple-element.123) | copy-start | bytes 3076
  27.8 328.2 %copy-start.6 = (f32[1,4,32,1024]{3,2,1,0:T(8,128)}, f32[1,4,32,1024]{3,2,1,0:T(8,128)S(1)}, u32[]{:S(2)}) copy-start(f32[1,4,32,1024]{3,2,1,0:T(8,128)S(1)} %get-tuple-element.16) | copy-start | bytes 1572868
  27.8 328.2 %copy-start.8 = (f32[4,32,1024]{2,1,0:T(8,128)}, f32[4,32,1024]{2,1,0:T(8,128)S(1)}, u32[]{:S(2)}) copy-start(f32[4,32,1024]{2,1,0:T(8,128)S(1)} %get-tuple-element.17) | copy-start | bytes 1572868
  36.3 7.6 %copy-start.47 = (f32[8,16,256]{2,1,0:T(8,128)S(1)}, f32[8,16,256]{2,1,0:T(8,128)}, u32[]{:S(2)}) copy-start(f32[8,16,256]{2,1,0:T(8,128)} %param.9) | copy-start | bytes 393220
  46.5 7.0 %collective-permute-start.2 = (f32[4,8,1,258]{3,1,2,0:T(8,128)S(1)}, f32[4,8,1,258]{3,1,2,0:T(8,128)S(1)}, u32[]{:S(2)}, u32[]{:S(2)}) collective-permute-start(f32[4,8,1,258]{3,1,2,0:T(8,128)S(1)} %get-tuple-element.89), channel_id=1, source_target_pairs={{0,1},{1,2},{2,3},{3,4},{4,5},{5,6},{6,7},{7,8},{8,9},{9,10},{10,1... | collective-permute-start | bytes 99080 | tf_op jit(solution)/shard_map/ppermute | solution.py:22
  50.0 6.0 %collective-permute-start.3 = (f32[4,8,1,258]{3,1,2,0:T(8,128)S(1)}, f32[4,8,1,258]{3,1,2,0:T(8,128)S(1)}, u32[]{:S(2)}, u32[]{:S(2)}) collective-permute-start(f32[4,8,1,258]{3,1,2,0:T(8,128)S(1)} %get-tuple-element.88), channel_id=1, source_target_pairs={{1,0},{2,1},{3,2},{4,3},{5,4},{6,5},{7,6},{8,7},{9,8},{10,9},{11,1... | collective-permute-start | bytes 99080 | tf_op jit(solution)/shard_map/ppermute | solution.py:24
  74.1 9.4 %copy-start.64 = (f32[3,8,8,32]{3,1,2,0:T(8,128)S(1)}, f32[3,8,8,32]{3,1,2,0:T(8,128)}, u32[]{:S(2)}) copy-start(f32[3,8,8,32]{3,1,2,0:T(8,128)} %slice.499) | copy-start | bytes 73732
  74.1 9.4 %copy-start.63 = (f32[3,8,8,32]{3,1,2,0:T(8,128)S(1)}, f32[3,8,8,32]{3,1,2,0:T(8,128)}, u32[]{:S(2)}) copy-start(f32[3,8,8,32]{3,1,2,0:T(8,128)} %slice.500) | copy-start | bytes 73732
  74.2 10.0 %copy-start.48 = (f32[1,8,16,256]{3,2,1,0:T(8,128)}, f32[1,8,16,256]{3,2,1,0:T(8,128)S(1)}, u32[]{:S(2)}) copy-start(f32[1,8,16,256]{3,2,1,0:T(8,128)S(1)} %copy.242) | copy-start | bytes 393220
  74.3 9.9 %copy-start.50 = (f32[1,8,16,256]{3,2,1,0:T(8,128)}, f32[1,8,16,256]{3,2,1,0:T(8,128)S(1)}, u32[]{:S(2)}) copy-start(f32[1,8,16,256]{3,2,1,0:T(8,128)S(1)} %copy.243) | copy-start | bytes 393220
  74.4 9.9 %copy-start.52 = (f32[1,8,16,256]{3,2,1,0:T(8,128)}, f32[1,8,16,256]{3,2,1,0:T(8,128)S(1)}, u32[]{:S(2)}) copy-start(f32[1,8,16,256]{3,2,1,0:T(8,128)S(1)} %copy.244) | copy-start | bytes 393220
  75.1 11.8 %copy-start.62 = (f32[3,8,8,32]{3,1,2,0:T(8,128)S(1)}, f32[3,8,8,32]{3,1,2,0:T(8,128)}, u32[]{:S(2)}) copy-start(f32[3,8,8,32]{3,1,2,0:T(8,128)} %slice.504) | copy-start | bytes 73732
  75.9 11.6 %copy-start.67 = (f32[4,8,1,258]{3,1,2,0:T(8,128)S(1)}, f32[4,8,1,258]{3,1,2,0:T(8,128)}, u32[]{:S(2)}) copy-start(f32[4,8,1,258]{3,1,2,0:T(8,128)} %copy-done.65) | copy-start | bytes 99076
  77.2 20.3 %collective-permute-start.4 = (f32[3,8,1,256]{3,1,2,0:T(8,128)}, f32[3,8,1,256]{3,1,2,0:T(8,128)}, u32[]{:S(2)}, u32[]{:S(2)}) collective-permute-start(f32[3,8,1,256]{3,1,2,0:T(8,128)} %copy.245), channel_id=1, source_target_pairs={{0,1},{1,2},{2,3},{3,4},{4,5},{5,6},{6,7},{7,8},{8,9},{9,10},{10,1... | collective-permute-start | bytes 73736 | tf_op jit(solution)/shard_map/ppermute | solution.py:22
  81.9 15.6 %collective-permute-start.5 = (f32[3,8,1,256]{3,1,2,0:T(8,128)}, f32[3,8,1,256]{3,1,2,0:T(8,128)}, u32[]{:S(2)}, u32[]{:S(2)}) collective-permute-start(f32[3,8,1,256]{3,1,2,0:T(8,128)} %copy.246), channel_id=1, source_target_pairs={{1,0},{2,1},{3,2},{4,3},{5,4},{6,5},{7,6},{8,7},{9,8},{10,9},{11,1... | collective-permute-start | bytes 73736 | tf_op jit(solution)/shard_map/ppermute | solution.py:24
  112.1 7.8 %copy-start.85 = (s32[128]{0:T(128)S(1)}, s32[128]{0:T(128)}, u32[]{:S(2)}) copy-start(s32[128]{0:T(128)} %fusion.138) | copy-start | bytes 1540
  124.3 22.2 %all-to-all-start = ((f32[32,4,768]{2,1,0:T(4,128)}), f32[32,4,768]{2,1,0:T(4,128)}, u32[]{:S(2)}, u32[]{:S(2)}) async-start(f32[32,4,768]{2,1,0:T(4,128)} %reshape.321), calls=%async_computation | async-start | bytes 786432 | tf_op jit(solution)/shard_map/all_to_all | solution.py:201
  146.5 71.5 %all-to-all-start.1 = ((f32[32,4,768]{2,1,0:T(4,128)}), f32[32,4,768]{2,1,0:T(4,128)}, u32[]{:S(2)}, u32[]{:S(2)}) async-start(f32[32,4,768]{2,1,0:T(4,128)} %reshape.327), calls=%async_computation.1 | async-start | bytes 786432 | tf_op jit(solution)/shard_map/all_to_all | solution.py:201
  193.8 6.0 %copy-start.18 = (f32[4,32,1024]{2,1,0:T(8,128)S(1)}, f32[4,32,1024]{2,1,0:T(8,128)}, u32[]{:S(2)}) copy-start(f32[4,32,1024]{2,1,0:T(8,128)} %get-tuple-element.90) | copy-start | bytes 1572868
  193.8 6.0 %copy-start.58 = (f32[4,3,32,1]{3,2,0,1:T(8,128)S(1)}, f32[4,3,32,1]{3,2,0,1:T(8,128)}, u32[]{:S(2)}) copy-start(f32[4,3,32,1]{3,2,0,1:T(8,128)} %get-tuple-element.64) | copy-start | bytes 4612
  193.8 6.0 %copy-start.59 = (f32[4,3,32,1]{3,2,0,1:T(8,128)S(1)}, f32[4,3,32,1]{3,2,0,1:T(8,128)}, u32[]{:S(2)}) copy-start(f32[4,3,32,1]{3,2,0,1:T(8,128)} %get-tuple-element.65) | copy-start | bytes 4612
  207.7 148.3 %copy-start.10 = (f32[1,4,32,1024]{3,2,1,0:T(8,128)}, f32[1,4,32,1024]{3,2,1,0:T(8,128)S(1)}, u32[]{:S(2)}) copy-start(f32[1,4,32,1024]{3,2,1,0:T(8,128)S(1)} %get-tuple-element.59) | copy-start | bytes 1572868
  218.0 85.2 %all-to-all-start.2 = ((f32[32,4,768]{2,1,0:T(4,128)}), f32[32,4,768]{2,1,0:T(4,128)S(1)}, u32[]{:S(2)}, u32[]{:S(2)}) async-start(f32[32,4,768]{2,1,0:T(4,128)} %reshape.333), calls=%async_computation.2 | async-start | bytes 786432 | tf_op jit(solution)/shard_map/all_to_all | solution.py:201
  303.2 75.3 %all-to-all-start.3 = ((f32[32,4,768]{2,1,0:T(4,128)}), f32[32,4,768]{2,1,0:T(4,128)}, u32[]{:S(2)}, u32[]{:S(2)}) async-start(f32[32,4,768]{2,1,0:T(4,128)} %reshape.339), calls=%async_computation.3 | async-start | bytes 786432 | tf_op jit(solution)/shard_map/all_to_all | solution.py:201
  350.0 6.0 %copy-start.60 = (f32[4,3,32,1]{3,2,0,1:T(8,128)S(1)}, f32[4,3,32,1]{3,2,0,1:T(8,128)}, u32[]{:S(2)}) copy-start(f32[4,3,32,1]{3,2,0,1:T(8,128)} %get-tuple-element.38) | copy-start | bytes 4612
  350.0 6.0 %copy-start.61 = (f32[4,3,32,1]{3,2,0,1:T(8,128)S(1)}, f32[4,3,32,1]{3,2,0,1:T(8,128)}, u32[]{:S(2)}) copy-start(f32[4,3,32,1]{3,2,0,1:T(8,128)} %get-tuple-element.39) | copy-start | bytes 4612
  350.0 6.0 %copy-start.77 = (pred[1024]{0:T(1024)(128)(4,1)S(1)}, pred[1024]{0:T(1024)(128)(4,1)}, u32[]{:S(2)}) copy-start(pred[1024]{0:T(1024)(128)(4,1)} %copy-done.75) | copy-start | bytes 3076
  350.0 6.0 %copy-start.80 = (pred[1024]{0:T(1024)(128)(4,1)S(1)}, pred[1024]{0:T(1024)(128)(4,1)}, u32[]{:S(2)}) copy-start(pred[1024]{0:T(1024)(128)(4,1)} %copy-done.78) | copy-start | bytes 3076
  350.0 6.0 %copy-start.83 = (pred[1024]{0:T(1024)(128)(4,1)S(1)}, pred[1024]{0:T(1024)(128)(4,1)}, u32[]{:S(2)}) copy-start(pred[1024]{0:T(1024)(128)(4,1)} %get-tuple-element.124) | copy-start | bytes 3076
  356.1 10.5 %copy-start.29 = (f32[4,32,1024]{2,1,0:T(8,128)S(1)}, f32[4,32,1024]{2,1,0:T(8,128)}, u32[]{:S(2)}) copy-start(f32[4,32,1024]{2,1,0:T(8,128)} %get-tuple-element.15) | copy-start | bytes 1572868
  356.1 10.5 %copy-start.31 = (f32[1,4,32,1024]{3,2,1,0:T(8,128)S(1)}, f32[1,4,32,1024]{3,2,1,0:T(8,128)}, u32[]{:S(2)}) copy-start(f32[1,4,32,1024]{3,2,1,0:T(8,128)} %copy-done.30) | copy-start | bytes 1572868
  356.1 10.5 %copy-start.33 = (f32[1,4,32,1024]{3,2,1,0:T(8,128)S(1)}, f32[1,4,32,1024]{3,2,1,0:T(8,128)}, u32[]{:S(2)}) copy-start(f32[1,4,32,1024]{3,2,1,0:T(8,128)} %copy-done.32) | copy-start | bytes 1572868
  356.1 10.5 %copy-start.35 = (f32[1,4,32,1024]{3,2,1,0:T(8,128)S(1)}, f32[1,4,32,1024]{3,2,1,0:T(8,128)}, u32[]{:S(2)}) copy-start(f32[1,4,32,1024]{3,2,1,0:T(8,128)} %copy-done.34) | copy-start | bytes 1572868
  356.1 10.5 %copy-start.42 = (f32[1,4,32,1024]{3,2,1,0:T(8,128)S(1)}, f32[1,4,32,1024]{3,2,1,0:T(8,128)}, u32[]{:S(2)}) copy-start(f32[1,4,32,1024]{3,2,1,0:T(8,128)} %get-tuple-element.12) | copy-start | bytes 1572868
  356.1 10.5 %copy-start.43 = (f32[4,32,1024]{2,1,0:T(8,128)S(1)}, f32[4,32,1024]{2,1,0:T(8,128)}, u32[]{:S(2)}) copy-start(f32[4,32,1024]{2,1,0:T(8,128)} %get-tuple-element.13) | copy-start | bytes 1572868
  412.1 6.1 %copy-start.19 = (f32[4,32,1024]{2,1,0:T(8,128)S(1)}, f32[4,32,1024]{2,1,0:T(8,128)}, u32[]{:S(2)}) copy-start(f32[4,32,1024]{2,1,0:T(8,128)} %get-tuple-element.90) | copy-start | bytes 1572868
  412.1 6.1 %copy-start.20 = (f32[4,32,1024]{2,1,0:T(8,128)S(1)}, f32[4,32,1024]{2,1,0:T(8,128)}, u32[]{:S(2)}) copy-start(f32[4,32,1024]{2,1,0:T(8,128)} %get-tuple-element.91) | copy-start | bytes 1572868
  412.1 6.1 %copy-start.21 = (f32[4,32,1024]{2,1,0:T(8,128)S(1)}, f32[4,32,1024]{2,1,0:T(8,128)}, u32[]{:S(2)}) copy-start(f32[4,32,1024]{2,1,0:T(8,128)} %get-tuple-element.92) | copy-start | bytes 1572868
  412.1 6.1 %copy-start.74 = (pred[1024]{0:T(1024)(128)(4,1)S(1)}, pred[1024]{0:T(1024)(128)(4,1)}, u32[]{:S(2)}) copy-start(pred[1024]{0:T(1024)(128)(4,1)} %copy-done.72) | copy-start | bytes 3076
  427.1 53.4 %copy-start.36 = (f32[4,3,32,1024]{3,2,1,0:T(8,128)}, f32[4,3,32,1024]{3,2,1,0:T(8,128)S(1)}, u32[]{:S(2)}) copy-start(f32[4,3,32,1024]{3,2,1,0:T(8,128)S(1)} %bitcast_add_fusion) | copy-start | bytes 4718596
  498.4 86.4 %copy-start.86 = (s32[64]{0:T(128)S(1)}, s32[64]{0:T(128)}, u32[]{:S(2)}) copy-start(s32[64]{0:T(128)} %sub.185) | copy-start | bytes 772
  590.4 6.7 %copy-start.1 = (s32[512,2]{0,1:T(2,128)S(1)}, s32[512,2]{0,1:T(2,128)}, u32[]{:S(2)}) copy-start(s32[512,2]{0,1:T(2,128)} %param.14) | copy-start | bytes 12292
  (49 other events, 133.1 us)
where the time goes:
time: 608 us; the launch traced here: 597 us
  local copies, waits for them, and re-layouts  357 us (59%)
  other arithmetic  87.3 us (14%)
  blocking collectives  85.9 us (14%)
  starting transfers between devices  55.6 us (9%)
  matrix products  7.74 us (1%)
    all_gather x1, blocking collectives, per_device(): portion = lax.all_gather(averages, 'af', axis=0, tiled=True)  85.9 us
    reshape x1, local copies, waits for them, and re-layouts, restrict(): shaped = fields.reshape(3, NZC, RATIO, BLK, RATIO, BLK, RATIO)  53.4 us
    another operation x12, local copies, waits for them, and re-layouts, patch_step(): jnp.tile(ghosts[1], (1, 1, edge_len))  39.5 us
    another operation x12, local copies, waits for them, and re-layouts, patch_step(): jnp.tile(ghosts[0], (1, 1, edge_len))  38.9 us
    all_to_all x4, starting transfers between devices, per_device(): lax.all_to_all(send_rows.reshape(af_count, slot_count, current.shape[1]),...  38.1 us
    add x5, other arithmetic, combine(): summed = summed + harmonic(conduct, coeffs) * (values - center)  35.9 us
    reshape x4, local copies, waits for them, and re-layouts, patch_step(): jnp.repeat(ghosts[2], edge_len, axis=-1)  23.6 us
    reshape x4, local copies, waits for them, and re-layouts, patch_step(): jnp.repeat(ghosts[3], edge_len, axis=-1)  23.6 us
  transfers between devices with their start and end apart: 10, of which 1 were waited for; matrix products, arithmetic and copies ran while one was open for 44% of the time, Pallas kernels for 0%

commit v1 on v0

--- a/solution.py
+++ b/solution.py
@@ -2,6 +2,7 @@
 import jax.numpy as jnp
 from jax import lax
 from jax.sharding import PartitionSpec as P
+from jax.lax import all_to_all, axis_size
 
 NZC = 8
 RATIO = 4
@@ -213,7 +214,15 @@
         cover, (af_index * block_cols, col_index * block_rows), (block_cols, block_rows)
     ).reshape(-1)
     wanted = cover_mine - group_base
-    portion = lax.all_gather(averages, "af", axis=0, tiled=True)
+    portion = jnp.concatenate(
+        all_to_all(
+            jnp.stack([averages for _ in range(axis_size("af"))], axis=0),
+            axis_name="af",
+            split_axis=0,
+            concat_axis=0,
+        ),
+        axis=0,
+    )
     selector = (wanted[:, None] == jnp.arange(portion.shape[0], dtype=jnp.int32)[None, :]).astype(
         jnp.float32
     )

time: 608 us -> 533 us (0.88)
  blocking collectives: 85.9 us -> 0 us
  waiting for transfers between devices: 2.21 us -> 11.5 us
  starting transfers between devices: 55.6 us -> 64 us
  local copies, waits for them, and re-layouts: 357 us -> 350 us
    all_gather x1 -> x0, blocking collectives: 85.9 us -> none  [per_device(): portion = lax.all_gather(averages, 'af', axis=0, tiled=True)]
    all_to_all x0 -> x1, waiting for transfers between devices: none -> 9.29 us  [per_device(): all_to_all(jnp.stack([averages for _ in range(axis_size('af'))], axis=0),...]
    all_to_all x0 -> x1, starting transfers between devices: none -> 8.41 us  [per_device(): all_to_all(jnp.stack([averages for _ in range(axis_size('af'))], axis=0),...]
  transfers between devices with their start and end apart: 10 -> 11, of which waited for: 1 -> 2; matrix products, arithmetic and copies ran while one was open for 44% -> 49% of each run, Pallas kernels for 0% -> 0%
where the time goes in v1:
time: 533 us; the launch traced here: 522 us
  local copies, waits for them, and re-layouts  350 us (66%)
  other arithmetic  86.8 us (16%)
  starting transfers between devices  64 us (12%)
  waiting for transfers between devices  11.5 us (2%)
  matrix products  7.8 us (1%)
    reshape x1, local copies, waits for them, and re-layouts, restrict(): shaped = fields.reshape(3, NZC, RATIO, BLK, RATIO, BLK, RATIO)  53.4 us
    another operation x12, local copies, waits for them, and re-layouts, patch_step(): jnp.tile(ghosts[1], (1, 1, edge_len))  39.5 us
    another operation x12, local copies, waits for them, and re-layouts, patch_step(): jnp.tile(ghosts[0], (1, 1, edge_len))  38.9 us
    all_to_all x4, starting transfers between devices, per_device(): lax.all_to_all(send_rows.reshape(af_count, slot_count, current.shape[1]),...  38.1 us
    add x5, other arithmetic, combine(): summed = summed + harmonic(conduct, coeffs) * (values - center)  36 us
    reshape x4, local copies, waits for them, and re-layouts, patch_step(): jnp.repeat(ghosts[3], edge_len, axis=-1)  23.6 us
    reshape x4, local copies, waits for them, and re-layouts, patch_step(): jnp.repeat(ghosts[2], edge_len, axis=-1)  23.6 us
    reduce_sum x1, other arithmetic, restrict(): return jnp.mean(shaped, axis=(2, 4, 6)).reshape(-1)  17.8 us
  transfers between devices with their start and end apart: 11, of which 2 were waited for; matrix products, arithmetic and copies ran while one was open for 49% of the time, Pallas kernels for 0%

profile of v1, /device:TPU:4, one launch (start us, length us, event | category | flops | bytes accessed | tf_op | source)
XLA Modules:
  0.0 522.5 jit_solution(9326713145646141320)
XLA Ops:
  4.6 5.1 collective-permute-start.1
  26.8 4.5 compare_select_fusion.10
  38.1 3.5 collective-permute-start.2
  52.8 3.1 slice.500
  58.9 3.1 slice.504
  68.8 4.1 collective-permute-start.4
  95.8 3.1 slice.532
  98.8 3.1 slice.533
  115.7 12.2 %all-to-all-start = ((f32[32,4,768]{2,1,0:T(4,128)}), f32[32,4,768]{2,1,0:T(4,128)}, u32[]{:S(2)}, u32[]{:S(2)}) async-start(f32[32,4,768]{2,1,0:T(4,128)} %reshape.376), calls=%async_computation | async-start | bytes 786432 | tf_op jit(solution)/shard_map/all_to_all | solution.py:202
  137.9 8.9 %all-to-all-start.1 = ((f32[32,4,768]{2,1,0:T(4,128)}), f32[32,4,768]{2,1,0:T(4,128)}, u32[]{:S(2)}, u32[]{:S(2)}) async-start(f32[32,4,768]{2,1,0:T(4,128)} %reshape.382), calls=%async_computation.1 | async-start | bytes 786432 | tf_op jit(solution)/shard_map/all_to_all | solution.py:202
  153.7 3.7 broadcast_in_dim.329
  157.4 5.9 %reshape.380 = f32[4,3,32,1024]{3,2,0,1:T(8,128)} reshape(f32[4,3,32,32,32]{4,3,2,0,1:T(8,128)} %broadcast_in_dim.329) | data formatting | bytes 3145728 | tf_op jit(solution)/shard_map/vmap()/reshape | solution.py:116
  163.4 3.7 broadcast_in_dim.332
  167.1 5.9 %reshape.381 = f32[4,3,32,1024]{3,2,0,1:T(8,128)} reshape(f32[4,3,32,32,32]{4,3,2,0,1:T(8,128)} %broadcast_in_dim.332) | data formatting | bytes 3145728 | tf_op jit(solution)/shard_map/vmap()/reshape | solution.py:122
  176.1 5.9 %tile.82 = f32[4,3,32,1024]{3,2,0,1:T(8,128)} reshape(f32[4,3,32,32,32]{4,3,2,0,1:T(8,128)} %tile.81) | data formatting | bytes 3145728 | tf_op jit(solution)/shard_map/vmap()/tile | solution.py:104
  185.2 6.0 %tile.85 = f32[4,3,32,1024]{3,2,0,1:T(8,128)} reshape(f32[4,3,32,32,32]{4,3,2,0,1:T(8,128)} %tile.84) | data formatting | bytes 3145728 | tf_op jit(solution)/shard_map/vmap()/tile | solution.py:110
  191.2 7.7 %fusion.5 = f32[4,3,32,1024]{3,2,0,1:T(8,128)S(1)} fusion(f32[4,3,32,1024]{3,2,0,1:T(8,128)} %tile.82, f32[4,3,32,32]{3,2,0,1:T(8,128)} %get-tuple-element.69, f32[4,3,32,992]{3,2,0,1:T(8,128)} %get-tuple-element.71, f32[4,3,32,1024]{3,2,0,1:T(8,128)} %tile.85, f32[4,3,32,992]{3,2,0,1:T(8,128)} %get-tuple-element.70, f32[4,3,32,32]{3,2,0,1:T(8,128)} %get-tuple-element.68, ...), kind=kLoop, calls=%fused_computation.8 | loop fusion | flops 9830400 | bytes 21925888 | tf_op jit(solution)/shard_map/vmap()/add | solution.py:41
  209.4 8.4 %all-to-all-start.2 = ((f32[32,4,768]{2,1,0:T(4,128)}), f32[32,4,768]{2,1,0:T(4,128)S(1)}, u32[]{:S(2)}, u32[]{:S(2)}) async-start(f32[32,4,768]{2,1,0:T(4,128)} %reshape.388), calls=%async_computation.2 | async-start | bytes 786432 | tf_op jit(solution)/shard_map/all_to_all | solution.py:202
  227.5 4.8 broadcast_in_dim.335
  232.3 5.9 %reshape.386 = f32[4,3,32,1024]{3,2,0,1:T(8,128)} reshape(f32[4,3,32,32,32]{4,3,2,0,1:T(8,128)} %broadcast_in_dim.335) | data formatting | bytes 3145728 | tf_op jit(solution)/shard_map/vmap()/reshape | solution.py:116
  239.9 4.8 broadcast_in_dim.336
  244.7 5.9 %reshape.387 = f32[4,3,32,1024]{3,2,0,1:T(8,128)} reshape(f32[4,3,32,32,32]{4,3,2,0,1:T(8,128)} %broadcast_in_dim.336) | data formatting | bytes 3145728 | tf_op jit(solution)/shard_map/vmap()/reshape | solution.py:122
  252.3 3.9 tile.87
  256.3 5.9 %tile.88 = f32[4,3,32,1024]{3,2,0,1:T(8,128)} reshape(f32[4,3,32,32,32]{4,3,2,0,1:T(8,128)} %tile.87) | data formatting | bytes 3145728 | tf_op jit(solution)/shard_map/vmap()/tile | solution.py:104
  263.9 3.9 tile.90
  267.8 5.9 %tile.91 = f32[4,3,32,1024]{3,2,0,1:T(8,128)} reshape(f32[4,3,32,32,32]{4,3,2,0,1:T(8,128)} %tile.90) | data formatting | bytes 3145728 | tf_op jit(solution)/shard_map/vmap()/tile | solution.py:110
  273.8 8.4 %fusion.21 = f32[4,3,32,1024]{3,2,0,1:T(8,128)S(1)} fusion(f32[4,3,32,1024]{3,2,0,1:T(8,128)} %tile.88, f32[4,3,32,32]{3,2,0,1:T(8,128)} %get-tuple-element.56, f32[4,3,32,992]{3,2,0,1:T(8,128)} %get-tuple-element.58, f32[4,3,32,1024]{3,2,0,1:T(8,128)} %tile.91, f32[4,3,32,992]{3,2,0,1:T(8,128)} %get-tuple-element.57, ...), kind=kLoop, calls=%fused_computation.29 | loop fusion | flops 12976128 | bytes 24547328 | tf_op jit(solution)/shard_map/vmap()/add | solution.py:41
  294.5 8.6 %all-to-all-start.3 = ((f32[32,4,768]{2,1,0:T(4,128)}), f32[32,4,768]{2,1,0:T(4,128)}, u32[]{:S(2)}, u32[]{:S(2)}) async-start(f32[32,4,768]{2,1,0:T(4,128)} %reshape.394), calls=%async_computation.3 | async-start | bytes 786432 | tf_op jit(solution)/shard_map/all_to_all | solution.py:202
  307.9 3.7 broadcast_in_dim.339
  311.6 5.9 %reshape.392 = f32[4,3,32,1024]{3,2,0,1:T(8,128)} reshape(f32[4,3,32,32,32]{4,3,2,0,1:T(8,128)} %broadcast_in_dim.339) | data formatting | bytes 3145728 | tf_op jit(solution)/shard_map/vmap()/reshape | solution.py:116
  318.5 3.7 broadcast_in_dim.340
  322.2 5.9 %reshape.393 = f32[4,3,32,1024]{3,2,0,1:T(8,128)} reshape(f32[4,3,32,32,32]{4,3,2,0,1:T(8,128)} %broadcast_in_dim.340) | data formatting | bytes 3145728 | tf_op jit(solution)/shard_map/vmap()/reshape | solution.py:122
  332.1 5.9 %tile.94 = f32[4,3,32,1024]{3,2,0,1:T(8,128)} reshape(f32[4,3,32,32,32]{4,3,2,0,1:T(8,128)} %tile.93) | data formatting | bytes 3145728 | tf_op jit(solution)/shard_map/vmap()/tile | solution.py:104
  341.2 6.0 %tile.97 = f32[4,3,32,1024]{3,2,0,1:T(8,128)} reshape(f32[4,3,32,32,32]{4,3,2,0,1:T(8,128)} %tile.96) | data formatting | bytes 3145728 | tf_op jit(solution)/shard_map/vmap()/tile | solution.py:110
  347.3 10.2 %fusion.37 = f32[4,3,32,1024]{3,2,0,1:T(8,128)S(1)} fusion(f32[4,3,32,1024]{3,2,0,1:T(8,128)} %tile.94, f32[4,3,32,32]{3,2,0,1:T(8,128)} %get-tuple-element.43, f32[4,3,32,992]{3,2,0,1:T(8,128)} %get-tuple-element.45, f32[4,3,32,1024]{3,2,0,1:T(8,128)} %tile.97, f32[4,3,32,992]{3,2,0,1:T(8,128)} %get-tuple-element.44, ...), kind=kLoop, calls=%fused_computation.50 | loop fusion | flops 16121856 | bytes 27168768 | tf_op jit(solution)/shard_map/vmap()/add | solution.py:41
  371.8 3.7 broadcast_in_dim.343
  375.5 5.9 %reshape.398 = f32[4,3,32,1024]{3,2,0,1:T(8,128)} reshape(f32[4,3,32,32,32]{4,3,2,0,1:T(8,128)} %broadcast_in_dim.343) | data formatting | bytes 3145728 | tf_op jit(solution)/shard_map/vmap()/reshape | solution.py:116
  381.5 3.7 broadcast_in_dim.344
  385.2 5.9 %reshape.399 = f32[4,3,32,1024]{3,2,0,1:T(8,128)} reshape(f32[4,3,32,32,32]{4,3,2,0,1:T(8,128)} %broadcast_in_dim.344) | data formatting | bytes 3145728 | tf_op jit(solution)/shard_map/vmap()/reshape | solution.py:122
  394.2 5.9 %tile.100 = f32[4,3,32,1024]{3,2,0,1:T(8,128)} reshape(f32[4,3,32,32,32]{4,3,2,0,1:T(8,128)} %tile.99) | data formatting | bytes 3145728 | tf_op jit(solution)/shard_map/vmap()/tile | solution.py:104
  403.2 6.1 %tile.103 = f32[4,3,32,1024]{3,2,0,1:T(8,128)} reshape(f32[4,3,32,32,32]{4,3,2,0,1:T(8,128)} %tile.102) | data formatting | bytes 3145728 | tf_op jit(solution)/shard_map/vmap()/tile | solution.py:110
  409.3 7.3 %fusion.50 = f32[4,3,32,1024]{3,2,0,1:T(8,128)S(1)} fusion(f32[4,3,32,1024]{3,2,0,1:T(8,128)} %tile.100, f32[4,3,32,1024]{3,2,0,1:T(8,128)} %tile.103, f32[4,3,32,1024]{3,2,0,1:T(8,128)} %reshape.398, f32[4,3,32,1024]{3,2,0,1:T(8,128)} %reshape.399, f32[4,32,1024]{2,1,0:T(8,128)} %get-tuple-element.95, f32[4,32,1024]{2,1,0:T(8,128)S(1)} %copy-done.21, ...), kind=kLoop, calls=%fused_computation.68 | loop fusion | flops 9830400 | bytes 21925888 | tf_op jit(solution)/shard_map/vmap()/add | solution.py:41
  418.2 53.4 %reshape.400 = f32[4,3,8,4,8,4,8,4]{7,6,5,4,3,2,1,0:T(8,128)} reshape(f32[4,3,32,1024]{3,2,1,0:T(8,128)S(1)} %bitcast_add_fusion) | data formatting | bytes 3145728 | tf_op jit(solution)/shard_map/vmap()/reshape | solution.py:137
  471.7 17.8 %reduce_sum.49 = f32[4,3,8,8,8]{4,3,2,1,0:T(8,128)S(1)} reduce(f32[4,3,8,4,8,4,8,4]{7,6,5,4,3,2,1,0:T(8,128)} %reshape.400, f32[]{:T(128)} %constant.94.clone.1), dimensions={3,5,7}, to_apply=%region_4.5 | reduce | flops 387072 | bytes 1597444 | tf_op jit(solution)/shard_map/vmap()/reduce_sum | solution.py:138
  490.7 8.4 %all-to-all-start.4 = ((f32[32,4,1536]{2,1,0:T(4,128)}), f32[32,4,1536]{2,1,0:T(4,128)S(1)}, u32[]{:S(2)}, u32[]{:S(2)}) async-start(f32[32,4,1536]{2,1,0:T(4,128)} %stack.178), calls=%async_computation.4 | async-start | bytes 1572864 | tf_op jit(solution)/shard_map/all_to_all | solution.py:218
  500.8 9.3 %all-to-all-done.4 = f32[32,4,1536]{2,1,0:T(4,128)S(1)} async-done(((f32[32,4,1536]{2,1,0:T(4,128)}), f32[32,4,1536]{2,1,0:T(4,128)S(1)}, u32[]{:S(2)}, u32[]{:S(2)}) %all-to-all-start.4) | async-done | bytes 786464 | tf_op jit(solution)/shard_map/all_to_all | solution.py:218
  511.6 4.0 copy.313
  515.6 5.7 %reshape.402 = f32[3,8,16,256]{3,2,1,0:T(8,128)S(1)} reshape(f32[3,8,2,8,32,8]{5,4,3,2,1,0:T(8,128)} %copy.313) | data formatting | bytes 786432 | tf_op jit(solution)/shard_map/reshape | solution.py:233
  (350 shorter events, 186.2 us)
Async XLA Ops:
  0.6 24.8 %copy-start = (s32[512,2]{0,1:T(2,128)S(1)}, s32[512,2]{0,1:T(2,128)}, u32[]{:S(2)}) copy-start(s32[512,2]{0,1:T(2,128)} %param.14) | copy-start | bytes 12292
  0.6 9.6 %copy-start.3 = (f32[4,32,1024]{2,1,0:T(8,128)S(1)}, f32[4,32,1024]{2,1,0:T(8,128)}, u32[]{:S(2)}) copy-start(f32[4,32,1024]{2,1,0:T(8,128)} %param.12) | copy-start | bytes 1572868
  2.6 32.9 %collective-permute-start = (f32[4,8,16,1]{3,2,1,0:T(8,128)}, f32[4,8,16,1]{3,2,1,0:T(8,128)}, u32[]{:S(2)}, u32[]{:S(2)}) collective-permute-start(f32[4,8,16,1]{3,2,1,0:T(8,128)} %get-tuple-element.108), channel_id=1, source_target_pairs={{0,32},{32,64},{64,96},{1,33},{33,65},{65,97},{2,34},{34,66},{66,9... | collective-permute-start | bytes 6152 | tf_op jit(solution)/shard_map/ppermute | solution.py:23
  4.6 31.0 %collective-permute-start.1 = (f32[4,8,16,1]{3,2,1,0:T(8,128)}, f32[4,8,16,1]{3,2,1,0:T(8,128)}, u32[]{:S(2)}, u32[]{:S(2)}) collective-permute-start(f32[4,8,16,1]{3,2,1,0:T(8,128)} %get-tuple-element.109), channel_id=1, source_target_pairs={{32,0},{64,32},{96,64},{33,1},{65,33},{97,65},{34,2},{66,34},{98,6... | collective-permute-start | bytes 6152 | tf_op jit(solution)/shard_map/ppermute | solution.py:25
  9.7 181.4 %copy-start.72 = (pred[1024]{0:T(1024)(128)(4,1)}, pred[1024]{0:T(1024)(128)(4,1)S(1)}, u32[]{:S(2)}) copy-start(pred[1024]{0:T(1024)(128)(4,1)S(1)} %get-tuple-element.121) | copy-start | bytes 3076
  9.7 181.4 %copy-start.75 = (pred[1024]{0:T(1024)(128)(4,1)}, pred[1024]{0:T(1024)(128)(4,1)S(1)}, u32[]{:S(2)}) copy-start(pred[1024]{0:T(1024)(128)(4,1)S(1)} %get-tuple-element.122) | copy-start | bytes 3076
  10.3 180.9 %copy-start.78 = (pred[1024]{0:T(1024)(128)(4,1)}, pred[1024]{0:T(1024)(128)(4,1)S(1)}, u32[]{:S(2)}) copy-start(pred[1024]{0:T(1024)(128)(4,1)S(1)} %get-tuple-element.123) | copy-start | bytes 3076
  25.4 321.8 %copy-start.6 = (f32[1,4,32,1024]{3,2,1,0:T(8,128)}, f32[1,4,32,1024]{3,2,1,0:T(8,128)S(1)}, u32[]{:S(2)}) copy-start(f32[1,4,32,1024]{3,2,1,0:T(8,128)S(1)} %get-tuple-element.16) | copy-start | bytes 1572868
  25.4 321.8 %copy-start.8 = (f32[4,32,1024]{2,1,0:T(8,128)}, f32[4,32,1024]{2,1,0:T(8,128)S(1)}, u32[]{:S(2)}) copy-start(f32[4,32,1024]{2,1,0:T(8,128)S(1)} %get-tuple-element.17) | copy-start | bytes 1572868
  38.1 7.0 %collective-permute-start.2 = (f32[4,8,1,258]{3,1,2,0:T(8,128)S(1)}, f32[4,8,1,258]{3,1,2,0:T(8,128)S(1)}, u32[]{:S(2)}, u32[]{:S(2)}) collective-permute-start(f32[4,8,1,258]{3,1,2,0:T(8,128)S(1)} %get-tuple-element.89), channel_id=1, source_target_pairs={{0,1},{1,2},{2,3},{3,4},{4,5},{5,6},{6,7},{7,8},{8,9},{9,10},{10,1... | collective-permute-start | bytes 99080 | tf_op jit(solution)/shard_map/ppermute | solution.py:23
  41.5 6.0 %collective-permute-start.3 = (f32[4,8,1,258]{3,1,2,0:T(8,128)S(1)}, f32[4,8,1,258]{3,1,2,0:T(8,128)S(1)}, u32[]{:S(2)}, u32[]{:S(2)}) collective-permute-start(f32[4,8,1,258]{3,1,2,0:T(8,128)S(1)} %get-tuple-element.88), channel_id=1, source_target_pairs={{1,0},{2,1},{3,2},{4,3},{5,4},{6,5},{7,6},{8,7},{9,8},{10,9},{11,1... | collective-permute-start | bytes 99080 | tf_op jit(solution)/shard_map/ppermute | solution.py:25
  65.6 9.4 %copy-start.64 = (f32[3,8,8,32]{3,1,2,0:T(8,128)S(1)}, f32[3,8,8,32]{3,1,2,0:T(8,128)}, u32[]{:S(2)}) copy-start(f32[3,8,8,32]{3,1,2,0:T(8,128)} %slice.499) | copy-start | bytes 73732
  65.7 9.4 %copy-start.63 = (f32[3,8,8,32]{3,1,2,0:T(8,128)S(1)}, f32[3,8,8,32]{3,1,2,0:T(8,128)}, u32[]{:S(2)}) copy-start(f32[3,8,8,32]{3,1,2,0:T(8,128)} %slice.500) | copy-start | bytes 73732
  65.8 10.0 %copy-start.48 = (f32[1,8,16,256]{3,2,1,0:T(8,128)}, f32[1,8,16,256]{3,2,1,0:T(8,128)S(1)}, u32[]{:S(2)}) copy-start(f32[1,8,16,256]{3,2,1,0:T(8,128)S(1)} %copy.241) | copy-start | bytes 393220
  65.8 9.9 %copy-start.50 = (f32[1,8,16,256]{3,2,1,0:T(8,128)}, f32[1,8,16,256]{3,2,1,0:T(8,128)S(1)}, u32[]{:S(2)}) copy-start(f32[1,8,16,256]{3,2,1,0:T(8,128)S(1)} %copy.242) | copy-start | bytes 393220
  65.9 9.8 %copy-start.52 = (f32[1,8,16,256]{3,2,1,0:T(8,128)}, f32[1,8,16,256]{3,2,1,0:T(8,128)S(1)}, u32[]{:S(2)}) copy-start(f32[1,8,16,256]{3,2,1,0:T(8,128)S(1)} %copy.243) | copy-start | bytes 393220
  66.6 11.8 %copy-start.62 = (f32[3,8,8,32]{3,1,2,0:T(8,128)S(1)}, f32[3,8,8,32]{3,1,2,0:T(8,128)}, u32[]{:S(2)}) copy-start(f32[3,8,8,32]{3,1,2,0:T(8,128)} %slice.504) | copy-start | bytes 73732
  67.4 11.6 %copy-start.67 = (f32[4,8,1,258]{3,1,2,0:T(8,128)S(1)}, f32[4,8,1,258]{3,1,2,0:T(8,128)}, u32[]{:S(2)}) copy-start(f32[4,8,1,258]{3,1,2,0:T(8,128)} %copy-done.65) | copy-start | bytes 99076
  68.8 20.2 %collective-permute-start.4 = (f32[3,8,1,256]{3,1,2,0:T(8,128)}, f32[3,8,1,256]{3,1,2,0:T(8,128)}, u32[]{:S(2)}, u32[]{:S(2)}) collective-permute-start(f32[3,8,1,256]{3,1,2,0:T(8,128)} %copy.244), channel_id=1, source_target_pairs={{0,1},{1,2},{2,3},{3,4},{4,5},{5,6},{6,7},{7,8},{8,9},{9,10},{10,1... | collective-permute-start | bytes 73736 | tf_op jit(solution)/shard_map/ppermute | solution.py:23
  73.4 15.6 %collective-permute-start.5 = (f32[3,8,1,256]{3,1,2,0:T(8,128)}, f32[3,8,1,256]{3,1,2,0:T(8,128)}, u32[]{:S(2)}, u32[]{:S(2)}) collective-permute-start(f32[3,8,1,256]{3,1,2,0:T(8,128)} %copy.245), channel_id=1, source_target_pairs={{1,0},{2,1},{3,2},{4,3},{5,4},{6,5},{7,6},{8,7},{9,8},{10,9},{11,1... | collective-permute-start | bytes 73736 | tf_op jit(solution)/shard_map/ppermute | solution.py:25
  115.7 22.2 %all-to-all-start = ((f32[32,4,768]{2,1,0:T(4,128)}), f32[32,4,768]{2,1,0:T(4,128)}, u32[]{:S(2)}, u32[]{:S(2)}) async-start(f32[32,4,768]{2,1,0:T(4,128)} %reshape.376), calls=%async_computation | async-start | bytes 786432 | tf_op jit(solution)/shard_map/all_to_all | solution.py:202
  137.9 71.4 %all-to-all-start.1 = ((f32[32,4,768]{2,1,0:T(4,128)}), f32[32,4,768]{2,1,0:T(4,128)}, u32[]{:S(2)}, u32[]{:S(2)}) async-start(f32[32,4,768]{2,1,0:T(4,128)} %reshape.382), calls=%async_computation.1 | async-start | bytes 786432 | tf_op jit(solution)/shard_map/all_to_all | solution.py:202
  185.1 6.0 %copy-start.18 = (f32[4,32,1024]{2,1,0:T(8,128)S(1)}, f32[4,32,1024]{2,1,0:T(8,128)}, u32[]{:S(2)}) copy-start(f32[4,32,1024]{2,1,0:T(8,128)} %get-tuple-element.90) | copy-start | bytes 1572868
  185.1 6.0 %copy-start.58 = (f32[4,3,32,1]{3,2,0,1:T(8,128)S(1)}, f32[4,3,32,1]{3,2,0,1:T(8,128)}, u32[]{:S(2)}) copy-start(f32[4,3,32,1]{3,2,0,1:T(8,128)} %get-tuple-element.64) | copy-start | bytes 4612
  185.2 6.1 %copy-start.59 = (f32[4,3,32,1]{3,2,0,1:T(8,128)S(1)}, f32[4,3,32,1]{3,2,0,1:T(8,128)}, u32[]{:S(2)}) copy-start(f32[4,3,32,1]{3,2,0,1:T(8,128)} %get-tuple-element.65) | copy-start | bytes 4612
  185.2 6.1 %copy-start.81 = (pred[1024]{0:T(1024)(128)(4,1)S(1)}, pred[1024]{0:T(1024)(128)(4,1)}, u32[]{:S(2)}) copy-start(pred[1024]{0:T(1024)(128)(4,1)} %get-tuple-element.124) | copy-start | bytes 3076
  199.1 148.1 %copy-start.10 = (f32[1,4,32,1024]{3,2,1,0:T(8,128)}, f32[1,4,32,1024]{3,2,1,0:T(8,128)S(1)}, u32[]{:S(2)}) copy-start(f32[1,4,32,1024]{3,2,1,0:T(8,128)S(1)} %get-tuple-element.59) | copy-start | bytes 1572868
  209.4 85.1 %all-to-all-start.2 = ((f32[32,4,768]{2,1,0:T(4,128)}), f32[32,4,768]{2,1,0:T(4,128)S(1)}, u32[]{:S(2)}, u32[]{:S(2)}) async-start(f32[32,4,768]{2,1,0:T(4,128)} %reshape.388), calls=%async_computation.2 | async-start | bytes 786432 | tf_op jit(solution)/shard_map/all_to_all | solution.py:202
  267.8 5.9 %copy-start.82 = (pred[1024]{0:T(1024)(128)(4,1)S(1)}, pred[1024]{0:T(1024)(128)(4,1)}, u32[]{:S(2)}) copy-start(pred[1024]{0:T(1024)(128)(4,1)} %get-tuple-element.124) | copy-start | bytes 3076
  294.5 75.2 %all-to-all-start.3 = ((f32[32,4,768]{2,1,0:T(4,128)}), f32[32,4,768]{2,1,0:T(4,128)}, u32[]{:S(2)}, u32[]{:S(2)}) async-start(f32[32,4,768]{2,1,0:T(4,128)} %reshape.394), calls=%async_computation.3 | async-start | bytes 786432 | tf_op jit(solution)/shard_map/all_to_all | solution.py:202
  341.2 6.0 %copy-start.60 = (f32[4,3,32,1]{3,2,0,1:T(8,128)S(1)}, f32[4,3,32,1]{3,2,0,1:T(8,128)}, u32[]{:S(2)}) copy-start(f32[4,3,32,1]{3,2,0,1:T(8,128)} %get-tuple-element.38) | copy-start | bytes 4612
  341.2 6.0 %copy-start.61 = (f32[4,3,32,1]{3,2,0,1:T(8,128)S(1)}, f32[4,3,32,1]{3,2,0,1:T(8,128)}, u32[]{:S(2)}) copy-start(f32[4,3,32,1]{3,2,0,1:T(8,128)} %get-tuple-element.39) | copy-start | bytes 4612
  341.2 6.0 %copy-start.77 = (pred[1024]{0:T(1024)(128)(4,1)S(1)}, pred[1024]{0:T(1024)(128)(4,1)}, u32[]{:S(2)}) copy-start(pred[1024]{0:T(1024)(128)(4,1)} %copy-done.75) | copy-start | bytes 3076
  341.2 6.0 %copy-start.80 = (pred[1024]{0:T(1024)(128)(4,1)S(1)}, pred[1024]{0:T(1024)(128)(4,1)}, u32[]{:S(2)}) copy-start(pred[1024]{0:T(1024)(128)(4,1)} %copy-done.78) | copy-start | bytes 3076
  341.2 6.0 %copy-start.83 = (pred[1024]{0:T(1024)(128)(4,1)S(1)}, pred[1024]{0:T(1024)(128)(4,1)}, u32[]{:S(2)}) copy-start(pred[1024]{0:T(1024)(128)(4,1)} %get-tuple-element.124) | copy-start | bytes 3076
  347.2 10.6 %copy-start.29 = (f32[4,32,1024]{2,1,0:T(8,128)S(1)}, f32[4,32,1024]{2,1,0:T(8,128)}, u32[]{:S(2)}) copy-start(f32[4,32,1024]{2,1,0:T(8,128)} %get-tuple-element.15) | copy-start | bytes 1572868
  347.2 10.6 %copy-start.31 = (f32[1,4,32,1024]{3,2,1,0:T(8,128)S(1)}, f32[1,4,32,1024]{3,2,1,0:T(8,128)}, u32[]{:S(2)}) copy-start(f32[1,4,32,1024]{3,2,1,0:T(8,128)} %copy-done.30) | copy-start | bytes 1572868
  347.2 10.6 %copy-start.33 = (f32[1,4,32,1024]{3,2,1,0:T(8,128)S(1)}, f32[1,4,32,1024]{3,2,1,0:T(8,128)}, u32[]{:S(2)}) copy-start(f32[1,4,32,1024]{3,2,1,0:T(8,128)} %copy-done.32) | copy-start | bytes 1572868
  347.2 10.6 %copy-start.35 = (f32[1,4,32,1024]{3,2,1,0:T(8,128)S(1)}, f32[1,4,32,1024]{3,2,1,0:T(8,128)}, u32[]{:S(2)}) copy-start(f32[1,4,32,1024]{3,2,1,0:T(8,128)} %copy-done.34) | copy-start | bytes 1572868
  347.3 10.6 %copy-start.42 = (f32[1,4,32,1024]{3,2,1,0:T(8,128)S(1)}, f32[1,4,32,1024]{3,2,1,0:T(8,128)}, u32[]{:S(2)}) copy-start(f32[1,4,32,1024]{3,2,1,0:T(8,128)} %get-tuple-element.12) | copy-start | bytes 1572868
  347.3 10.6 %copy-start.43 = (f32[4,32,1024]{2,1,0:T(8,128)S(1)}, f32[4,32,1024]{2,1,0:T(8,128)}, u32[]{:S(2)}) copy-start(f32[4,32,1024]{2,1,0:T(8,128)} %get-tuple-element.13) | copy-start | bytes 1572868
  403.2 6.1 %copy-start.19 = (f32[4,32,1024]{2,1,0:T(8,128)S(1)}, f32[4,32,1024]{2,1,0:T(8,128)}, u32[]{:S(2)}) copy-start(f32[4,32,1024]{2,1,0:T(8,128)} %get-tuple-element.90) | copy-start | bytes 1572868
  403.2 6.1 %copy-start.20 = (f32[4,32,1024]{2,1,0:T(8,128)S(1)}, f32[4,32,1024]{2,1,0:T(8,128)}, u32[]{:S(2)}) copy-start(f32[4,32,1024]{2,1,0:T(8,128)} %get-tuple-element.91) | copy-start | bytes 1572868
  403.2 6.1 %copy-start.21 = (f32[4,32,1024]{2,1,0:T(8,128)S(1)}, f32[4,32,1024]{2,1,0:T(8,128)}, u32[]{:S(2)}) copy-start(f32[4,32,1024]{2,1,0:T(8,128)} %get-tuple-element.92) | copy-start | bytes 1572868
  403.2 6.1 %copy-start.74 = (pred[1024]{0:T(1024)(128)(4,1)S(1)}, pred[1024]{0:T(1024)(128)(4,1)}, u32[]{:S(2)}) copy-start(pred[1024]{0:T(1024)(128)(4,1)} %copy-done.72) | copy-start | bytes 3076
  418.2 53.4 %copy-start.36 = (f32[4,3,32,1024]{3,2,1,0:T(8,128)}, f32[4,3,32,1024]{3,2,1,0:T(8,128)S(1)}, u32[]{:S(2)}) copy-start(f32[4,3,32,1024]{3,2,1,0:T(8,128)S(1)} %bitcast_add_fusion) | copy-start | bytes 4718596
  490.7 19.4 %all-to-all-start.4 = ((f32[32,4,1536]{2,1,0:T(4,128)}), f32[32,4,1536]{2,1,0:T(4,128)S(1)}, u32[]{:S(2)}, u32[]{:S(2)}) async-start(f32[32,4,1536]{2,1,0:T(4,128)} %stack.178), calls=%async_computation.4 | async-start | bytes 1572864 | tf_op jit(solution)/shard_map/all_to_all | solution.py:218
  515.6 6.7 %copy-start.1 = (s32[512,2]{0,1:T(2,128)S(1)}, s32[512,2]{0,1:T(2,128)}, u32[]{:S(2)}) copy-start(s32[512,2]{0,1:T(2,128)} %param.14) | copy-start | bytes 12292
  (47 other events, 120.1 us)
